TPU v7x, 32 devices: a whole 2x2x4 slice. The times are simulated.
32 devices in a mesh: leaf: 32 (over z, y, x, core).
Axes of the slice: x: 2, y: 2, z: 4, core: 2. Of those that a mesh axis runs over, the one named last changes fastest.
Arguments:
- points: float32 [16, 65536], P(None, 'leaf'), may hold values from -6 to 6
- charges: float32 [16, 65536], P(None, 'leaf'), may hold values from -0.6 to 0.6
- near_list: int32 [128, 32], P('leaf'), may hold values from 0 to 127, as said below
- near_count: int32 [128], P('leaf'), may hold values from 1 to 32, as said below
- leaf_basis: float32 [65536, 256], P('leaf'), may hold values from -0.75 to 0.75
- device_basis: float32 [32768, 256], P('leaf'), may hold values from -0.1875 to 0.1875
- device_skeleton: int32 [32, 256], P('leaf'), may hold values from 0 to 2047, as said below
- group_basis: float32 [1024, 2048], P(None, 'leaf'), may hold values from -0.1875 to 0.1875
- group_skeleton: int32 [2048], P('leaf'), may hold values from 0 to 1023, as said below
- cluster_basis: float32 [1024, 512], P(None, 'leaf'), may hold values from -0.1875 to 0.1875
- cluster_skeleton: int32 [512], P('leaf'), may hold values from 0 to 1023, as said below
Outputs:
- potentials: float32 [16, 65536], P(None, 'leaf')
Inputs may be any that keep to these rules, and one draw needn't show every extreme that they name: `near_list`: row l names leaves whose devices lie at most 8 devices from leaf l's device; its first entry is l, its first near_count[l] entries are distinct, and the later entries repeat l. Only the first near_count[l] entries of leaf l's list count. `device_skeleton`: each row holds distinct indices into its device's points. `group_skeleton`: entries g * 256 to (g + 1) * 256 - 1 are distinct indices into the 1024 skeleton points of group g's four devices, side by side in device order. `cluster_skeleton`: entries c * 256 to (c + 1) * 256 - 1 are distinct indices into the 1024 skeleton points of cluster c's four groups, side by side in group order.
All inputs are finite; a program needn't handle non-finite values.
Results may differ from a plain program's by a relative error of at most 0.0034.
Values sent between devices are 32-bit elements; how exact they have to be, the bound alone decides.
A program may use at most 64 MiB of HBM per device.

v0:
```python
import jax
import jax.numpy as jnp
from jax import lax
from jax.sharding import PartitionSpec as P

F = 16
R = 16
LEAF = 512
S = 256
REACH = 8
LEAVES_DEV = 4


inverse_spread = 1.0 / 16.0
exact_mode = lax.Precision.HIGHEST
tiles_per_step = 8


def passed_along(value, axis, steps):
    count = lax.axis_size(axis)
    leading, last = (max(0, -steps), min(count, count - steps))
    return lax.ppermute(value, axis, [(source, source + steps) for source in range(leading, last)])


def partner_2(value, axis, stride):
    mask = 2**stride
    pairs = [(source, source ^ mask) for source in range(lax.axis_size(axis))]
    return lax.ppermute(value, axis, pairs)


def kernel_of(left_points, right_points):
    cross_terms = jnp.dot(
        left_points.T, right_points, precision=exact_mode, preferred_element_type=jnp.float32
    )
    left_square = jnp.sum(left_points * left_points, axis=0)
    right_square = jnp.sum(right_points * right_points, axis=0)
    return jnp.exp(
        -(left_square[:, None] + right_square[None, :] - 2.0 * cross_terms) * inverse_spread
    )


def near_window(payload):
    pieces = []
    for offset in range(-REACH, REACH + 1):
        if offset == 0:
            pieces.append(payload)
        else:
            pieces.append(passed_along(payload, "leaf", -offset))
    return jnp.concatenate(pieces, axis=1)


def near_field(points, window, near_list, near_count):
    width_leaves = (2 * REACH + 1) * LEAVES_DEV
    stacked = window.reshape(F + R, width_leaves, LEAF)
    first_leaf = (lax.axis_index("leaf") - REACH) * LEAVES_DEV
    local_ids = near_list - first_leaf

    def block_term(leaf_index, step_index):
        picked = lax.dynamic_slice(
            local_ids, (leaf_index, step_index * tiles_per_step), (1, tiles_per_step)
        )[0]
        slots = step_index * tiles_per_step + jnp.arange(tiles_per_step, dtype=jnp.int32)
        live = (slots < near_count[leaf_index]).astype(jnp.float32)
        source = jnp.take(stacked, picked, axis=1)
        source_points = source[:F].reshape(F, tiles_per_step * LEAF)
        source_charges = (
            (source[F:] * live[None, :, None])
            .astype(jnp.bfloat16)
            .reshape(R, tiles_per_step * LEAF)
        )
        target = lax.dynamic_slice_in_dim(points, leaf_index * LEAF, LEAF, 1)
        kernel_tile = kernel_of(target, source_points).astype(jnp.bfloat16)
        return lax.dot_general(
            source_charges,
            kernel_tile,
            (((1,), (1,)), ((), ())),
            preferred_element_type=jnp.float32,
        )

    initial = jnp.zeros((R, LEAVES_DEV * LEAF), jnp.float32)

    def leaf_step(leaf_index, running):
        needed = (near_count[leaf_index] + tiles_per_step - 1) // tiles_per_step

        def inner_step(step_index, partial_sum):
            return partial_sum + block_term(leaf_index, step_index)

        leaf_block = lax.fori_loop(0, needed, inner_step, jnp.zeros((R, LEAF), jnp.float32))
        return lax.dynamic_update_slice_in_dim(running, leaf_block, leaf_index * LEAF, 1)

    return lax.fori_loop(0, LEAVES_DEV, leaf_step, initial)


def collect_pairwise(payload, bit_list):
    position = lax.axis_index("leaf")
    for bit in bit_list:
        partner = partner_2(payload, "leaf", bit)
        upper_half = position >> bit & 1 == 1
        payload = jnp.where(
            upper_half,
            jnp.concatenate([partner, payload], 1),
            jnp.concatenate([payload, partner], 1),
        )
    return payload


def spread_pairwise(partial_sum, bit_list):
    position = lax.axis_index("leaf")
    for bit in bit_list:
        half = partial_sum.shape[1] // 2
        lower_columns = partial_sum[:, :half]
        upper_columns = partial_sum[:, half:]
        upper_half = position >> bit & 1 == 1
        outgoing = jnp.where(upper_half, lower_columns, upper_columns)
        incoming = partner_2(outgoing, "leaf", bit)
        partial_sum = jnp.where(upper_half, upper_columns, lower_columns) + incoming
    return partial_sum


def right_product(left_matrix, right_matrix):
    return lax.dot_general(
        left_matrix,
        right_matrix,
        (((1,), (1,)), ((), ())),
        precision=exact_mode,
        preferred_element_type=jnp.float32,
    )


def shards(
    points,
    charges,
    near_list,
    near_count,
    leaf_basis,
    device_basis,
    device_skeleton,
    group_basis,
    group_skeleton,
    cluster_basis,
    cluster_skeleton,
):
    payload = jnp.concatenate([points, charges], axis=0)
    window = near_window(payload)
    near = near_field(points, window, near_list, near_count)
    position = lax.axis_index("leaf")
    leaf_blocks = leaf_basis.reshape(LEAVES_DEV, LEAF, S)
    leaf_weights = jnp.einsum(
        "lps,rlp->rls", leaf_blocks, charges.reshape(R, LEAVES_DEV, LEAF), precision=exact_mode
    )
    device_weights = jnp.dot(
        leaf_weights.reshape(R, LEAVES_DEV * S), device_basis, precision=exact_mode
    )
    device_points = jnp.take(points, device_skeleton[0], axis=1)
    device_payload = jnp.concatenate([device_points, device_weights], axis=0)
    group_stack = collect_pairwise(device_payload, (0, 1))
    quarter_weights = jnp.dot(group_stack[F:], group_basis, precision=exact_mode)
    quarter_points = jnp.take(group_stack[:F], group_skeleton, axis=1)
    quarter_payload = jnp.concatenate([quarter_points, quarter_weights], axis=0)
    cluster_stack = collect_pairwise(quarter_payload, (0, 1, 2, 3))
    cluster_points = cluster_stack[:F]
    cluster_weights = cluster_stack[F:]
    part_weights = jnp.dot(cluster_weights, cluster_basis, precision=exact_mode)
    part_points = jnp.take(cluster_points, cluster_skeleton, axis=1)
    all_nodes = lax.all_gather(
        jnp.concatenate([part_points, part_weights], axis=0), "leaf", axis=1, tiled=True
    )
    cluster_of = jnp.arange(all_nodes.shape[1]) // S
    top_kernel = kernel_of(part_points, all_nodes[:F]) * (cluster_of != position // 16)[None, :]
    top_part = right_product(all_nodes[F:], top_kernel)
    group_of = jnp.arange(4 * S) // S
    side_kernel = (
        kernel_of(quarter_points, cluster_points) * (group_of != position % 16 // 4)[None, :]
    )
    side_part = right_product(cluster_weights, side_kernel)
    from_top = right_product(top_part, cluster_basis)
    down_group = side_part + spread_pairwise(from_top, (3, 2, 1, 0))
    from_group = right_product(down_group, group_basis)
    down_device = spread_pairwise(from_group, (1, 0))
    down_leaves = right_product(down_device, device_basis)
    far_field = jnp.einsum(
        "lps,rls->rlp", leaf_blocks, down_leaves.reshape(R, LEAVES_DEV, S), precision=exact_mode
    )
    return near + far_field.reshape(R, LEAVES_DEV * LEAF)


def solution(mesh):
    return jax.shard_map(
        shards,
        mesh=mesh,
        in_specs=(
            P(None, "leaf"),
            P(None, "leaf"),
            P("leaf", None),
            P("leaf"),
            P("leaf", None),
            P("leaf", None),
            P("leaf", None),
            P(None, "leaf"),
            P("leaf"),
            P(None, "leaf"),
            P("leaf"),
        ),
        out_specs=P(None, "leaf"),
        check_vma=False,
    )
```

profile of v0, /device:TPU:2, one launch (start us, length us, event | category | flops | bytes accessed | tf_op | source)
XLA Modules:
  0.0 341.0 jit_solution(14831466100846820593)
XLA Ops:
  3.3 4.2 %collective-permute-start = (f32[32,2048]{1,0:T(8,128)}, f32[32,2048]{1,0:T(8,128)}, u32[]{:S(2)}, u32[]{:S(2)}) collective-permute-start(f32[32,2048]{1,0:T(8,128)} %constant_dynamic-update-slice_fusion.1), channel_id=1, source_target_pairs={{0,8},{1,9},{2,10},{3,11},{4,12},{5,13},{6,14},{7,15},{8,16},{9,17... | collective-permute-start | bytes 786440 | tf_op jit(solution)/shard_map/ppermute | solution.py:22
  10.1 4.4 %collective-permute-start.2 = (f32[32,2048]{1,0:T(8,128)}, f32[32,2048]{1,0:T(8,128)}, u32[]{:S(2)}, u32[]{:S(2)}) collective-permute-start(f32[32,2048]{1,0:T(8,128)} %constant_dynamic-update-slice_fusion.1), channel_id=1, source_target_pairs={{0,6},{1,7},{2,8},{3,9},{4,10},{5,11},{6,12},{7,13},{8,14},{9,15},... | collective-permute-start | bytes 786440 | tf_op jit(solution)/shard_map/ppermute | solution.py:22
  49.9 38.7 %all_gather.3 = f32[32,512]{0,1:T(8,128)S(1)} all-gather(f32[32,16]{0,1:T(8,128)S(1)} %pad_maximum_fusion.2), channel_id=1, replica_groups=mesh['leaf'=32] {'leaf'}, dimensions={1}, use_global_device_ids=true | all-gather | bytes 67584 | tf_op jit(solution)/shard_map/all_gather | solution.py:165
  119.2 5.0 %collective-permute-done.9 = f32[32,2048]{1,0:T(8,128)S(1)} collective-permute-done((f32[32,2048]{1,0:T(8,128)}, f32[32,2048]{1,0:T(8,128)S(1)}, u32[]{:S(2)}, u32[]{:S(2)}) %collective-permute-start.9) | collective-permute-done | bytes 262176 | tf_op jit(solution)/shard_map/ppermute | solution.py:22
  127.5 9.5 %collective-permute-done.11 = f32[32,2048]{1,0:T(8,128)S(1)} collective-permute-done((f32[32,2048]{1,0:T(8,128)}, f32[32,2048]{1,0:T(8,128)S(1)}, u32[]{:S(2)}, u32[]{:S(2)}) %collective-permute-start.11) | collective-permute-done | bytes 262176 | tf_op jit(solution)/shard_map/ppermute | solution.py:22
  140.8 7.2 %collective-permute-start.24 = (f32[16,128]{1,0:T(8,128)S(1)}, f32[16,128]{1,0:T(8,128)S(1)}, u32[]{:S(2)}, u32[]{:S(2)}) collective-permute-start(f32[16,128]{1,0:T(8,128)S(1)} %slice_select_fusion.5), channel_id=1, source_target_pairs={{0,2},{1,3},{2,0},{3,1},{4,6},{5,7},{6,4},{7,5},{8,10},{9,11},{10,... | collective-permute-start | bytes 24584 | tf_op jit(solution)/shard_map/ppermute | solution.py:28
  159.6 176.6 %while.57 = (s32[]{:T(128)}, f32[16,2048]{1,0:T(8,128)S(1)}, s32[4]{0:T(128)S(1)}, f32[16,2048]{1,0:T(8,128)S(1)}, s32[4,32]{1,0:T(4,128)S(1)}, /*index=5*/f32[3...) while((s32[]{:T(128)}, f32[16,2048]{1,0:T(8,128)S(1)}, ...), condition=%wide.region_5.6_spmd, body=%wide.region_0.5_spmd.sunk | while | flops 482759296 | bytes 12919736 | solution.py:91
  160.9 26.4 %while.58 = (s32[]{:T(128)}, f32[16,512]{1,0:T(8,128)S(1)}, s32[]{:T(128)}, s32[4,32]{1,0:T(4,128)S(1)}, s32[]{:T(128)}, /*index=5*/f32[32,68,512]{2,0,1:T(8,128...) while((s32[]{:T(128)}, f32[16,512]{1,0:T(8,128)S(1)}, ...), condition=%wide.region_4.4_spmd, body=%wide.region_2.3_spmd.sunk | while | flops 482743392 | bytes 12753331 | solution.py:88
  164.9 8.6 %fusion.86 = bf16[512,4096]{0,1:T(8,128)(2,1)S(1)} fusion(f32[16,4096]{1,0:T(8,128)S(1)} %bitcast.111, f32[16,512]{1,0:T(8,128)S(1)} %get-tuple-element.541, f32[4096]{0:T(1024)S(1)} %bitcast.114, f32[512]{0:T(512)S(1)} %get-tuple-element.540), kind=kOutput, calls=%fused_computation.8.clone.1 | convolution fusion | flops 415236096 | bytes 4507648 | tf_op jit(solution)/shard_map/while/body/eval_jaxpr/while/body/dot_general | solution.py:32
  178.0 8.6 %fusion.86 = bf16[512,4096]{0,1:T(8,128)(2,1)S(1)} fusion(f32[16,4096]{1,0:T(8,128)S(1)} %bitcast.111, f32[16,512]{1,0:T(8,128)S(1)} %get-tuple-element.541, f32[4096]{0:T(1024)S(1)} %bitcast.114, f32[512]{0:T(512)S(1)} %get-tuple-element.540), kind=kOutput, calls=%fused_computation.8.clone.1 | convolution fusion | flops 415236096 | bytes 4507648 | tf_op jit(solution)/shard_map/while/body/eval_jaxpr/while/body/dot_general | solution.py:32
  188.6 39.5 %while.58 = (s32[]{:T(128)}, f32[16,512]{1,0:T(8,128)S(1)}, s32[]{:T(128)}, s32[4,32]{1,0:T(4,128)S(1)}, s32[]{:T(128)}, /*index=5*/f32[32,68,512]{2,0,1:T(8,128...) while((s32[]{:T(128)}, f32[16,512]{1,0:T(8,128)S(1)}, ...), condition=%wide.region_4.4_spmd, body=%wide.region_2.3_spmd.sunk | while | flops 482743392 | bytes 12753331 | solution.py:88
  192.5 8.6 %fusion.86 = bf16[512,4096]{0,1:T(8,128)(2,1)S(1)} fusion(f32[16,4096]{1,0:T(8,128)S(1)} %bitcast.111, f32[16,512]{1,0:T(8,128)S(1)} %get-tuple-element.541, f32[4096]{0:T(1024)S(1)} %bitcast.114, f32[512]{0:T(512)S(1)} %get-tuple-element.540), kind=kOutput, calls=%fused_computation.8.clone.1 | convolution fusion | flops 415236096 | bytes 4507648 | tf_op jit(solution)/shard_map/while/body/eval_jaxpr/while/body/dot_general | solution.py:32
  205.7 8.6 %fusion.86 = bf16[512,4096]{0,1:T(8,128)(2,1)S(1)} fusion(f32[16,4096]{1,0:T(8,128)S(1)} %bitcast.111, f32[16,512]{1,0:T(8,128)S(1)} %get-tuple-element.541, f32[4096]{0:T(1024)S(1)} %bitcast.114, f32[512]{0:T(512)S(1)} %get-tuple-element.540), kind=kOutput, calls=%fused_computation.8.clone.1 | convolution fusion | flops 415236096 | bytes 4507648 | tf_op jit(solution)/shard_map/while/body/eval_jaxpr/while/body/dot_general | solution.py:32
  218.9 8.6 %fusion.86 = bf16[512,4096]{0,1:T(8,128)(2,1)S(1)} fusion(f32[16,4096]{1,0:T(8,128)S(1)} %bitcast.111, f32[16,512]{1,0:T(8,128)S(1)} %get-tuple-element.541, f32[4096]{0:T(1024)S(1)} %bitcast.114, f32[512]{0:T(512)S(1)} %get-tuple-element.540), kind=kOutput, calls=%fused_computation.8.clone.1 | convolution fusion | flops 415236096 | bytes 4507648 | tf_op jit(solution)/shard_map/while/body/eval_jaxpr/while/body/dot_general | solution.py:32
  229.5 52.7 %while.58 = (s32[]{:T(128)}, f32[16,512]{1,0:T(8,128)S(1)}, s32[]{:T(128)}, s32[4,32]{1,0:T(4,128)S(1)}, s32[]{:T(128)}, /*index=5*/f32[32,68,512]{2,0,1:T(8,128...) while((s32[]{:T(128)}, f32[16,512]{1,0:T(8,128)S(1)}, ...), condition=%wide.region_4.4_spmd, body=%wide.region_2.3_spmd.sunk | while | flops 482743392 | bytes 12753331 | solution.py:88
  233.4 8.6 %fusion.86 = bf16[512,4096]{0,1:T(8,128)(2,1)S(1)} fusion(f32[16,4096]{1,0:T(8,128)S(1)} %bitcast.111, f32[16,512]{1,0:T(8,128)S(1)} %get-tuple-element.541, f32[4096]{0:T(1024)S(1)} %bitcast.114, f32[512]{0:T(512)S(1)} %get-tuple-element.540), kind=kOutput, calls=%fused_computation.8.clone.1 | convolution fusion | flops 415236096 | bytes 4507648 | tf_op jit(solution)/shard_map/while/body/eval_jaxpr/while/body/dot_general | solution.py:32
  246.6 8.6 %fusion.86 = bf16[512,4096]{0,1:T(8,128)(2,1)S(1)} fusion(f32[16,4096]{1,0:T(8,128)S(1)} %bitcast.111, f32[16,512]{1,0:T(8,128)S(1)} %get-tuple-element.541, f32[4096]{0:T(1024)S(1)} %bitcast.114, f32[512]{0:T(512)S(1)} %get-tuple-element.540), kind=kOutput, calls=%fused_computation.8.clone.1 | convolution fusion | flops 415236096 | bytes 4507648 | tf_op jit(solution)/shard_map/while/body/eval_jaxpr/while/body/dot_general | solution.py:32
  259.7 8.6 %fusion.86 = bf16[512,4096]{0,1:T(8,128)(2,1)S(1)} fusion(f32[16,4096]{1,0:T(8,128)S(1)} %bitcast.111, f32[16,512]{1,0:T(8,128)S(1)} %get-tuple-element.541, f32[4096]{0:T(1024)S(1)} %bitcast.114, f32[512]{0:T(512)S(1)} %get-tuple-element.540), kind=kOutput, calls=%fused_computation.8.clone.1 | convolution fusion | flops 415236096 | bytes 4507648 | tf_op jit(solution)/shard_map/while/body/eval_jaxpr/while/body/dot_general | solution.py:32
  272.9 8.6 %fusion.86 = bf16[512,4096]{0,1:T(8,128)(2,1)S(1)} fusion(f32[16,4096]{1,0:T(8,128)S(1)} %bitcast.111, f32[16,512]{1,0:T(8,128)S(1)} %get-tuple-element.541, f32[4096]{0:T(1024)S(1)} %bitcast.114, f32[512]{0:T(512)S(1)} %get-tuple-element.540), kind=kOutput, calls=%fused_computation.8.clone.1 | convolution fusion | flops 415236096 | bytes 4507648 | tf_op jit(solution)/shard_map/while/body/eval_jaxpr/while/body/dot_general | solution.py:32
  283.5 52.7 %while.58 = (s32[]{:T(128)}, f32[16,512]{1,0:T(8,128)S(1)}, s32[]{:T(128)}, s32[4,32]{1,0:T(4,128)S(1)}, s32[]{:T(128)}, /*index=5*/f32[32,68,512]{2,0,1:T(8,128...) while((s32[]{:T(128)}, f32[16,512]{1,0:T(8,128)S(1)}, ...), condition=%wide.region_4.4_spmd, body=%wide.region_2.3_spmd.sunk | while | flops 482743392 | bytes 12753331 | solution.py:88
  287.4 8.6 %fusion.86 = bf16[512,4096]{0,1:T(8,128)(2,1)S(1)} fusion(f32[16,4096]{1,0:T(8,128)S(1)} %bitcast.111, f32[16,512]{1,0:T(8,128)S(1)} %get-tuple-element.541, f32[4096]{0:T(1024)S(1)} %bitcast.114, f32[512]{0:T(512)S(1)} %get-tuple-element.540), kind=kOutput, calls=%fused_computation.8.clone.1 | convolution fusion | flops 415236096 | bytes 4507648 | tf_op jit(solution)/shard_map/while/body/eval_jaxpr/while/body/dot_general | solution.py:32
  300.6 8.6 %fusion.86 = bf16[512,4096]{0,1:T(8,128)(2,1)S(1)} fusion(f32[16,4096]{1,0:T(8,128)S(1)} %bitcast.111, f32[16,512]{1,0:T(8,128)S(1)} %get-tuple-element.541, f32[4096]{0:T(1024)S(1)} %bitcast.114, f32[512]{0:T(512)S(1)} %get-tuple-element.540), kind=kOutput, calls=%fused_computation.8.clone.1 | convolution fusion | flops 415236096 | bytes 4507648 | tf_op jit(solution)/shard_map/while/body/eval_jaxpr/while/body/dot_general | solution.py:32
  313.8 8.6 %fusion.86 = bf16[512,4096]{0,1:T(8,128)(2,1)S(1)} fusion(f32[16,4096]{1,0:T(8,128)S(1)} %bitcast.111, f32[16,512]{1,0:T(8,128)S(1)} %get-tuple-element.541, f32[4096]{0:T(1024)S(1)} %bitcast.114, f32[512]{0:T(512)S(1)} %get-tuple-element.540), kind=kOutput, calls=%fused_computation.8.clone.1 | convolution fusion | flops 415236096 | bytes 4507648 | tf_op jit(solution)/shard_map/while/body/eval_jaxpr/while/body/dot_general | solution.py:32
  326.9 8.6 %fusion.86 = bf16[512,4096]{0,1:T(8,128)(2,1)S(1)} fusion(f32[16,4096]{1,0:T(8,128)S(1)} %bitcast.111, f32[16,512]{1,0:T(8,128)S(1)} %get-tuple-element.541, f32[4096]{0:T(1024)S(1)} %bitcast.114, f32[512]{0:T(512)S(1)} %get-tuple-element.540), kind=kOutput, calls=%fused_computation.8.clone.1 | convolution fusion | flops 415236096 | bytes 4507648 | tf_op jit(solution)/shard_map/while/body/eval_jaxpr/while/body/dot_general | solution.py:32
  (313 shorter events, 156.0 us)
Async XLA Ops:
  3.3 92.8 %collective-permute-start = (f32[32,2048]{1,0:T(8,128)}, f32[32,2048]{1,0:T(8,128)}, u32[]{:S(2)}, u32[]{:S(2)}) collective-permute-start(f32[32,2048]{1,0:T(8,128)} %constant_dynamic-update-slice_fusion.1), channel_id=1, source_target_pairs={{0,8},{1,9},{2,10},{3,11},{4,12},{5,13},{6,14},{7,15},{8,16},{9,17... | collective-permute-start | bytes 786440 | tf_op jit(solution)/shard_map/ppermute | solution.py:22
  7.5 92.5 %collective-permute-start.1 = (f32[32,2048]{1,0:T(8,128)}, f32[32,2048]{1,0:T(8,128)}, u32[]{:S(2)}, u32[]{:S(2)}) collective-permute-start(f32[32,2048]{1,0:T(8,128)} %constant_dynamic-update-slice_fusion.1), channel_id=1, source_target_pairs={{0,7},{1,8},{2,9},{3,10},{4,11},{5,12},{6,13},{7,14},{8,15},{9,16}... | collective-permute-start | bytes 786440 | tf_op jit(solution)/shard_map/ppermute | solution.py:22
  10.1 94.1 %collective-permute-start.2 = (f32[32,2048]{1,0:T(8,128)}, f32[32,2048]{1,0:T(8,128)}, u32[]{:S(2)}, u32[]{:S(2)}) collective-permute-start(f32[32,2048]{1,0:T(8,128)} %constant_dynamic-update-slice_fusion.1), channel_id=1, source_target_pairs={{0,6},{1,7},{2,8},{3,9},{4,10},{5,11},{6,12},{7,13},{8,14},{9,15},... | collective-permute-start | bytes 786440 | tf_op jit(solution)/shard_map/ppermute | solution.py:22
  14.5 92.7 %collective-permute-start.3 = (f32[32,2048]{1,0:T(8,128)}, f32[32,2048]{1,0:T(8,128)}, u32[]{:S(2)}, u32[]{:S(2)}) collective-permute-start(f32[32,2048]{1,0:T(8,128)} %constant_dynamic-update-slice_fusion.1), channel_id=1, source_target_pairs={{0,5},{1,6},{2,7},{3,8},{4,9},{5,10},{6,11},{7,12},{8,13},{9,14},{... | collective-permute-start | bytes 786440 | tf_op jit(solution)/shard_map/ppermute | solution.py:22
  28.7 4.4 %collective-permute-start.17 = (f32[32,512]{1,0:T(8,128)S(1)}, f32[32,512]{1,0:T(8,128)S(1)}, u32[]{:S(2)}, u32[]{:S(2)}) collective-permute-start(f32[32,512]{1,0:T(8,128)S(1)} %maximum_select_fusion.2), channel_id=1, source_target_pairs={{0,2},{1,3},{2,0},{3,1},{4,6},{5,7},{6,4},{7,5},{8,10},{9,11},{10,... | collective-permute-start | bytes 196616 | tf_op jit(solution)/shard_map/ppermute | solution.py:28
  35.8 3.7 %collective-permute-start.19 = (f32[32,128]{1,0:T(8,128)S(1)}, f32[32,128]{1,0:T(8,128)S(1)}, u32[]{:S(2)}, u32[]{:S(2)}) collective-permute-start(f32[32,128]{1,0:T(8,128)S(1)} %maximum_select_fusion.5), channel_id=1, source_target_pairs={{0,2},{1,3},{2,0},{3,1},{4,6},{5,7},{6,4},{7,5},{8,10},{9,11},{10,... | collective-permute-start | bytes 49160 | tf_op jit(solution)/shard_map/ppermute | solution.py:28
  39.5 3.9 %collective-permute-start.20 = (f32[32,256]{1,0:T(8,128)S(1)}, f32[32,256]{1,0:T(8,128)S(1)}, u32[]{:S(2)}, u32[]{:S(2)}) collective-permute-start(f32[32,256]{1,0:T(8,128)S(1)} %maximum_select_fusion.4), channel_id=1, source_target_pairs={{0,4},{1,5},{2,6},{3,7},{4,0},{5,1},{6,2},{7,3},{8,12},{9,13},{10,... | collective-permute-start | bytes 98312 | tf_op jit(solution)/shard_map/ppermute | solution.py:28
  43.4 4.3 %collective-permute-start.21 = (f32[32,512]{1,0:T(8,128)S(1)}, f32[32,512]{1,0:T(8,128)S(1)}, u32[]{:S(2)}, u32[]{:S(2)}) collective-permute-start(f32[32,512]{1,0:T(8,128)S(1)} %maximum_select_fusion.3), channel_id=1, source_target_pairs={{0,8},{1,9},{2,10},{3,11},{4,12},{5,13},{6,14},{7,15},{8,0},{9,1},... | collective-permute-start | bytes 196616 | tf_op jit(solution)/shard_map/ppermute | solution.py:28
  90.8 4.0 %collective-permute-start.22 = (f32[16,512]{1,0:T(8,128)S(1)}, f32[16,512]{1,0:T(8,128)S(1)}, u32[]{:S(2)}, u32[]{:S(2)}) collective-permute-start(f32[16,512]{1,0:T(8,128)S(1)} %slice_select_fusion.1), channel_id=1, source_target_pairs={{0,8},{1,9},{2,10},{3,11},{4,12},{5,13},{6,14},{7,15},{8,0},{9,1},... | collective-permute-start | bytes 98312 | tf_op jit(solution)/shard_map/ppermute | solution.py:28
  94.8 17.0 %collective-permute-start.4 = (f32[32,2048]{1,0:T(8,128)}, f32[32,2048]{1,0:T(8,128)S(1)}, u32[]{:S(2)}, u32[]{:S(2)}) collective-permute-start(f32[32,2048]{1,0:T(8,128)} %constant_dynamic-update-slice_fusion.1), channel_id=1, source_target_pairs={{0,4},{1,5},{2,6},{3,7},{4,8},{5,9},{6,10},{7,11},{8,12},{9,13},{1... | collective-permute-start | bytes 786440 | tf_op jit(solution)/shard_map/ppermute | solution.py:22
  96.1 17.6 %collective-permute-start.5 = (f32[32,2048]{1,0:T(8,128)}, f32[32,2048]{1,0:T(8,128)S(1)}, u32[]{:S(2)}, u32[]{:S(2)}) collective-permute-start(f32[32,2048]{1,0:T(8,128)} %constant_dynamic-update-slice_fusion.1), channel_id=1, source_target_pairs={{0,3},{1,4},{2,5},{3,6},{4,7},{5,8},{6,9},{7,10},{8,11},{9,12},{10... | collective-permute-start | bytes 786440 | tf_op jit(solution)/shard_map/ppermute | solution.py:22
  100.0 15.1 %collective-permute-start.6 = (f32[32,2048]{1,0:T(8,128)}, f32[32,2048]{1,0:T(8,128)S(1)}, u32[]{:S(2)}, u32[]{:S(2)}) collective-permute-start(f32[32,2048]{1,0:T(8,128)} %constant_dynamic-update-slice_fusion.1), channel_id=1, source_target_pairs={{0,2},{1,3},{2,4},{3,5},{4,6},{5,7},{6,8},{7,9},{8,10},{9,11},{10,... | collective-permute-start | bytes 786440 | tf_op jit(solution)/shard_map/ppermute | solution.py:22
  104.3 12.2 %collective-permute-start.7 = (f32[32,2048]{1,0:T(8,128)}, f32[32,2048]{1,0:T(8,128)S(1)}, u32[]{:S(2)}, u32[]{:S(2)}) collective-permute-start(f32[32,2048]{1,0:T(8,128)} %constant_dynamic-update-slice_fusion.1), channel_id=1, source_target_pairs={{0,1},{1,2},{2,3},{3,4},{4,5},{5,6},{6,7},{7,8},{8,9},{9,10},{10,1... | collective-permute-start | bytes 786440 | tf_op jit(solution)/shard_map/ppermute | solution.py:22
  107.2 10.7 %collective-permute-start.8 = (f32[32,2048]{1,0:T(8,128)}, f32[32,2048]{1,0:T(8,128)S(1)}, u32[]{:S(2)}, u32[]{:S(2)}) collective-permute-start(f32[32,2048]{1,0:T(8,128)} %constant_dynamic-update-slice_fusion.1), channel_id=1, source_target_pairs={{1,0},{2,1},{3,2},{4,3},{5,4},{6,5},{7,6},{8,7},{9,8},{10,9},{11,1... | collective-permute-start | bytes 786440 | tf_op jit(solution)/shard_map/ppermute | solution.py:22
  111.8 12.3 %collective-permute-start.9 = (f32[32,2048]{1,0:T(8,128)}, f32[32,2048]{1,0:T(8,128)S(1)}, u32[]{:S(2)}, u32[]{:S(2)}) collective-permute-start(f32[32,2048]{1,0:T(8,128)} %constant_dynamic-update-slice_fusion.1), channel_id=1, source_target_pairs={{2,0},{3,1},{4,2},{5,3},{6,4},{7,5},{8,6},{9,7},{10,8},{11,9},{12,... | collective-permute-start | bytes 786440 | tf_op jit(solution)/shard_map/ppermute | solution.py:22
  113.8 12.2 %collective-permute-start.10 = (f32[32,2048]{1,0:T(8,128)}, f32[32,2048]{1,0:T(8,128)S(1)}, u32[]{:S(2)}, u32[]{:S(2)}) collective-permute-start(f32[32,2048]{1,0:T(8,128)} %constant_dynamic-update-slice_fusion.1), channel_id=1, source_target_pairs={{3,0},{4,1},{5,2},{6,3},{7,4},{8,5},{9,6},{10,7},{11,8},{12,9},{13... | collective-permute-start | bytes 786440 | tf_op jit(solution)/shard_map/ppermute | solution.py:22
  115.1 21.9 %collective-permute-start.11 = (f32[32,2048]{1,0:T(8,128)}, f32[32,2048]{1,0:T(8,128)S(1)}, u32[]{:S(2)}, u32[]{:S(2)}) collective-permute-start(f32[32,2048]{1,0:T(8,128)} %constant_dynamic-update-slice_fusion.1), channel_id=1, source_target_pairs={{4,0},{5,1},{6,2},{7,3},{8,4},{9,5},{10,6},{11,7},{12,8},{13,9},{1... | collective-permute-start | bytes 786440 | tf_op jit(solution)/shard_map/ppermute | solution.py:22
  116.4 20.7 %collective-permute-start.12 = (f32[32,2048]{1,0:T(8,128)}, f32[32,2048]{1,0:T(8,128)S(1)}, u32[]{:S(2)}, u32[]{:S(2)}) collective-permute-start(f32[32,2048]{1,0:T(8,128)} %constant_dynamic-update-slice_fusion.1), channel_id=1, source_target_pairs={{5,0},{6,1},{7,2},{8,3},{9,4},{10,5},{11,6},{12,7},{13,8},{14,9},{... | collective-permute-start | bytes 786440 | tf_op jit(solution)/shard_map/ppermute | solution.py:22
  117.8 30.1 %collective-permute-start.13 = (f32[32,2048]{1,0:T(8,128)}, f32[32,2048]{1,0:T(8,128)S(1)}, u32[]{:S(2)}, u32[]{:S(2)}) collective-permute-start(f32[32,2048]{1,0:T(8,128)} %constant_dynamic-update-slice_fusion.1), channel_id=1, source_target_pairs={{6,0},{7,1},{8,2},{9,3},{10,4},{11,5},{12,6},{13,7},{14,8},{15,9},... | collective-permute-start | bytes 786440 | tf_op jit(solution)/shard_map/ppermute | solution.py:22
  124.1 26.1 %collective-permute-start.14 = (f32[32,2048]{1,0:T(8,128)}, f32[32,2048]{1,0:T(8,128)S(1)}, u32[]{:S(2)}, u32[]{:S(2)}) collective-permute-start(f32[32,2048]{1,0:T(8,128)} %constant_dynamic-update-slice_fusion.1), channel_id=1, source_target_pairs={{7,0},{8,1},{9,2},{10,3},{11,4},{12,5},{13,6},{14,7},{15,8},{16,9}... | collective-permute-start | bytes 786440 | tf_op jit(solution)/shard_map/ppermute | solution.py:22
  126.0 30.2 %collective-permute-start.15 = (f32[32,2048]{1,0:T(8,128)}, f32[32,2048]{1,0:T(8,128)S(1)}, u32[]{:S(2)}, u32[]{:S(2)}) collective-permute-start(f32[32,2048]{1,0:T(8,128)} %constant_dynamic-update-slice_fusion.1), channel_id=1, source_target_pairs={{8,0},{9,1},{10,2},{11,3},{12,4},{13,5},{14,6},{15,7},{16,8},{17,9... | collective-permute-start | bytes 786440 | tf_op jit(solution)/shard_map/ppermute | solution.py:22
  140.8 8.9 %collective-permute-start.24 = (f32[16,128]{1,0:T(8,128)S(1)}, f32[16,128]{1,0:T(8,128)S(1)}, u32[]{:S(2)}, u32[]{:S(2)}) collective-permute-start(f32[16,128]{1,0:T(8,128)S(1)} %slice_select_fusion.5), channel_id=1, source_target_pairs={{0,2},{1,3},{2,0},{3,1},{4,6},{5,7},{6,4},{7,5},{8,10},{9,11},{10,... | collective-permute-start | bytes 24584 | tf_op jit(solution)/shard_map/ppermute | solution.py:28
  151.5 7.4 %collective-permute-start.26 = (f32[16,512]{1,0:T(8,128)S(1)}, f32[16,512]{1,0:T(8,128)S(1)}, u32[]{:S(2)}, u32[]{:S(2)}) collective-permute-start(f32[16,512]{1,0:T(8,128)S(1)} %slice_select_fusion), channel_id=1, source_target_pairs={{0,2},{1,3},{2,0},{3,1},{4,6},{5,7},{6,4},{7,5},{8,10},{9,11},{10,... | collective-permute-start | bytes 98312 | tf_op jit(solution)/shard_map/ppermute | solution.py:28
  159.6 176.6 %collective-permute-start.27 = (f32[16,256]{1,0:T(8,128)}, f32[16,256]{1,0:T(8,128)}, u32[]{:S(2)}, u32[]{:S(2)}) collective-permute-start(f32[16,256]{1,0:T(8,128)} %slice_select_fusion.2), channel_id=1, source_target_pairs={{0,1},{1,0},{2,3},{3,2},{4,5},{5,4},{6,7},{7,6},{8,9},{9,8},{10,11... | collective-permute-start | bytes 49160 | tf_op jit(solution)/shard_map/ppermute | solution.py:28
  (15 other events, 528.0 us)
where the time goes:
time: 343 us; the launch traced here: 341 us
  matrix products  131 us (38%)
  local copies, waits for them, and re-layouts  57.6 us (17%)
  starting transfers between devices  51.4 us (15%)
  waiting for transfers between devices  41.6 us (12%)
  blocking collectives  38.7 us (11%)
  other arithmetic  16.3 us (5%)
  loops' own time  3.57 us (1%)
    dot_general x15, matrix products, kernel_of(): jnp.dot(left_points.T, right_points, precision=exact_mode, preferred_elem...  113 us
    all_gather x1, blocking collectives, shards(): lax.all_gather(jnp.concatenate([part_points, part_weights], axis=0), 'lea...  38.7 us
    gather x13, local copies, waits for them, and re-layouts, block_term(): source = jnp.take(stacked, picked, axis=1)  37.1 us
    ppermute x16, starting transfers between devices, passed_along(): lax.ppermute(value, axis, [(source, source + steps) for source in range(l...  36.8 us
    ppermute x12, waiting for transfers between devices, partner_2(): return lax.ppermute(value, axis, pairs)  23.4 us
    ppermute x16, waiting for transfers between devices, passed_along(): lax.ppermute(value, axis, [(source, source + steps) for source in range(l...  18.3 us
    ppermute x12, starting transfers between devices, partner_2(): return lax.ppermute(value, axis, pairs)  14.5 us
    dot_general x13, matrix products, block_term(): lax.dot_general(source_charges, kernel_tile, (((1,), (1,)), ((), ())), pr...  8.36 us
  transfers between devices with their start and end apart: 28, of which 16 were waited for; matrix products, arithmetic and copies ran while one was open for 58% of the time, Pallas kernels for 0%

commit v1 on v0

--- a/solution.py
+++ b/solution.py
@@ -1,6 +1,10 @@
+import math
+
 import jax
 import jax.numpy as jnp
 from jax import lax
+from jax.experimental import pallas as pl
+from jax.experimental.pallas import tpu as pltpu
 from jax.sharding import PartitionSpec as P
 
 F = 16
@@ -13,7 +17,6 @@
 
 inverse_spread = 1.0 / 16.0
 exact_mode = lax.Precision.HIGHEST
-tiles_per_step = 8
 
 
 def passed_along(value, axis, steps):
@@ -46,49 +49,98 @@
             pieces.append(payload)
         else:
             pieces.append(passed_along(payload, "leaf", -offset))
-    return jnp.concatenate(pieces, axis=1)
-
-
-def near_field(points, window, near_list, near_count):
-    width_leaves = (2 * REACH + 1) * LEAVES_DEV
-    stacked = window.reshape(F + R, width_leaves, LEAF)
-    first_leaf = (lax.axis_index("leaf") - REACH) * LEAVES_DEV
-    local_ids = near_list - first_leaf
-
-    def block_term(leaf_index, step_index):
-        picked = lax.dynamic_slice(
-            local_ids, (leaf_index, step_index * tiles_per_step), (1, tiles_per_step)
-        )[0]
-        slots = step_index * tiles_per_step + jnp.arange(tiles_per_step, dtype=jnp.int32)
-        live = (slots < near_count[leaf_index]).astype(jnp.float32)
-        source = jnp.take(stacked, picked, axis=1)
-        source_points = source[:F].reshape(F, tiles_per_step * LEAF)
-        source_charges = (
-            (source[F:] * live[None, :, None])
-            .astype(jnp.bfloat16)
-            .reshape(R, tiles_per_step * LEAF)
+    return jnp.stack(pieces, axis=0)
+
+
+def split3(value):
+    high = value.astype(jnp.bfloat16)
+    rest = value - high.astype(jnp.float32)
+    middle = rest.astype(jnp.bfloat16)
+    low = (rest - middle.astype(jnp.float32)).astype(jnp.bfloat16)
+    return high, middle, low
+
+
+def norm_rows(squares, first):
+    high, middle, low = (piece.astype(jnp.float32) for piece in split3(squares))
+    row = lax.broadcasted_iota(jnp.int32, (16, squares.shape[1]), 0)
+    ones = 3 - first
+    block = jnp.where((row >= ones) & (row < ones + 3), 1.0, 0.0)
+    block = jnp.where(row == first, high, block)
+    block = jnp.where(row == first + 1, middle, block)
+    return jnp.where(row == first + 2, low, block)
+
+
+def near_kernel(list_ref, count_ref, points_ref, window_ref, far_ref, out_ref, source, charge, target):
+    leaf = source.shape[2]
+    leaves_dev = points_ref.shape[1] // leaf
+    scale = inverse_spread * math.log2(math.e)
+
+    def prepare(device, carry):
+        for inner in range(leaves_dev):
+            columns = slice(inner * leaf, (inner + 1) * leaf)
+            block = window_ref[device, 0:F, columns]
+            slot = device * leaves_dev + inner
+            high, middle, low = split3(block)
+            squares = jnp.sum(block * block, axis=0, keepdims=True) * (-scale)
+            norms = norm_rows(squares, 3).astype(jnp.bfloat16)
+            pieces = (high, middle, high, low, high, middle, norms, jnp.zeros_like(norms))
+            for place, piece in enumerate(pieces):
+                source[slot, place * 16 : (place + 1) * 16, :] = piece
+            charge[slot] = window_ref[device, F : F + R, columns].astype(jnp.bfloat16)
+        return carry
+
+    lax.fori_loop(0, window_ref.shape[0], prepare, 0)
+
+    for inner in range(leaves_dev):
+        columns = slice(inner * leaf, (inner + 1) * leaf)
+        block = points_ref[:, columns]
+        high, middle, low = (p.astype(jnp.float32) for p in split3(block * (2.0 * scale)))
+        squares = jnp.sum(block * block, axis=0, keepdims=True) * (-scale)
+        norms = norm_rows(squares, 0)
+        stacked = jnp.concatenate(
+            [high, high, middle, high, low, middle, norms, jnp.zeros_like(norms)], axis=0
         )
-        target = lax.dynamic_slice_in_dim(points, leaf_index * LEAF, LEAF, 1)
-        kernel_tile = kernel_of(target, source_points).astype(jnp.bfloat16)
-        return lax.dot_general(
-            source_charges,
-            kernel_tile,
-            (((1,), (1,)), ((), ())),
-            preferred_element_type=jnp.float32,
-        )
-
-    initial = jnp.zeros((R, LEAVES_DEV * LEAF), jnp.float32)
-
-    def leaf_step(leaf_index, running):
-        needed = (near_count[leaf_index] + tiles_per_step - 1) // tiles_per_step
-
-        def inner_step(step_index, partial_sum):
-            return partial_sum + block_term(leaf_index, step_index)
-
-        leaf_block = lax.fori_loop(0, needed, inner_step, jnp.zeros((R, LEAF), jnp.float32))
-        return lax.dynamic_update_slice_in_dim(running, leaf_block, leaf_index * LEAF, 1)
-
-    return lax.fori_loop(0, LEAVES_DEV, leaf_step, initial)
+        target[...] = stacked.T.astype(jnp.bfloat16)
+        count = count_ref[inner]
+
+        def two_tiles(step, running):
+            for side in range(2):
+                slot = step * 2 + side
+                picked = list_ref[inner, slot]
+                live = (slot < count).astype(jnp.float32)
+                power = jnp.dot(target[...], source[picked], preferred_element_type=jnp.float32)
+                tile = jnp.exp2(power).astype(jnp.bfloat16)
+                weights = (charge[picked].astype(jnp.float32) * live).astype(jnp.bfloat16)
+                running = running + lax.dot_general(
+                    weights, tile, (((1,), (1,)), ((), ())), preferred_element_type=jnp.float32
+                )
+            return running
+
+        total = lax.fori_loop(0, (count + 1) // 2, two_tiles, jnp.zeros((R, leaf), jnp.float32))
+        out_ref[:, columns] = total + far_ref[:, columns]
+
+
+def near_field(points, window, near_list, near_count, far):
+    devices, _, width = window.shape
+    leaves_dev = near_list.shape[0]
+    leaf = width // leaves_dev
+    first_leaf = (lax.axis_index("leaf") - REACH) * leaves_dev
+    slots = devices * leaves_dev
+    vmem = pl.BlockSpec(memory_space=pltpu.VMEM)
+    smem = pl.BlockSpec(memory_space=pltpu.SMEM)
+    return pl.pallas_call(
+        near_kernel,
+        out_shape=jax.ShapeDtypeStruct((R, width), jnp.float32),
+        in_specs=[smem, smem, vmem, vmem, vmem],
+        out_specs=vmem,
+        scratch_shapes=[
+            pltpu.VMEM((slots, 128, leaf), jnp.bfloat16),
+            pltpu.VMEM((slots, R, leaf), jnp.bfloat16),
+            pltpu.VMEM((leaf, 128), jnp.bfloat16),
+        ],
+        compiler_params=pltpu.CompilerParams(vmem_limit_bytes=48 * 1024 * 1024),
+        name="near_tiles",
+    )(near_list - first_leaf, near_count, points, window, far)
 
 
 def collect_pairwise(payload, bit_list):
@@ -142,7 +194,6 @@
 ):
     payload = jnp.concatenate([points, charges], axis=0)
     window = near_window(payload)
-    near = near_field(points, window, near_list, near_count)
     position = lax.axis_index("leaf")
     leaf_blocks = leaf_basis.reshape(LEAVES_DEV, LEAF, S)
     leaf_weights = jnp.einsum(
@@ -181,7 +232,8 @@
     far_field = jnp.einsum(
         "lps,rls->rlp", leaf_blocks, down_leaves.reshape(R, LEAVES_DEV, S), precision=exact_mode
     )
-    return near + far_field.reshape(R, LEAVES_DEV * LEAF)
+    far_field = far_field.reshape(R, LEAVES_DEV * LEAF)
+    return near_field(points, window, near_list, near_count, far_field)
 
 
 def solution(mesh):

time: 343 us -> 208 us (0.61)
  the two profiles are of different devices: /device:TPU:2 before, /device:TPU:3 now
where the time goes in v1:
time: 208 us; the launch traced here: 212 us
  starting transfers between devices  59.6 us (29%)
  Pallas kernels  43.1 us (21%)
  blocking collectives  42.3 us (20%)
  waiting for transfers between devices  26.9 us (13%)
  local copies, waits for them, and re-layouts  20.6 us (10%)
  matrix products  11.7 us (6%)
  other arithmetic  7.05 us (3%)
    pallas_call x1, Pallas kernels, near_field(): pl.pallas_call(near_kernel, out_shape=jax.ShapeDtypeStruct((R, width), jn...  43.1 us
    all_gather x1, blocking collectives, shards(): lax.all_gather(jnp.concatenate([part_points, part_weights], axis=0), 'lea...  42.3 us
    ppermute x16, starting transfers between devices, passed_along(): lax.ppermute(value, axis, [(source, source + steps) for source in range(l...  39.6 us
    ppermute x12, starting transfers between devices, partner_2(): return lax.ppermute(value, axis, pairs)  20 us
    ppermute x12, waiting for transfers between devices, partner_2(): return lax.ppermute(value, axis, pairs)  18.3 us
    unnamed x38, local copies, waits for them, and re-layouts  9.05 us
    ppermute x16, waiting for transfers between devices, passed_along(): lax.ppermute(value, axis, [(source, source + steps) for source in range(l...  8.67 us
  transfers between devices with their start and end apart: 28, of which 14 were waited for; matrix products, arithmetic and copies ran while one was open for 16% of the time, Pallas kernels for 0%

profile of v1, /device:TPU:3, one launch (start us, length us, event | category | flops | bytes accessed | tf_op | source)
XLA Modules:
  0.0 211.9 jit_solution(4194336999732380599)
XLA Ops:
  3.3 3.9 %collective-permute-start = (f32[32,2048]{1,0:T(8,128)}, f32[32,2048]{1,0:T(8,128)}, u32[]{:S(2)}, u32[]{:S(2)}) collective-permute-start(f32[32,2048]{1,0:T(8,128)} %constant_dynamic-update-slice_fusion), channel_id=1, source_target_pairs={{0,8},{1,9},{2,10},{3,11},{4,12},{5,13},{6,14},{7,15},{8,16},{9,17... | collective-permute-start | bytes 786440 | tf_op jit(solution)/shard_map/ppermute | solution.py:25
  7.2 4.1 %collective-permute-start.1 = (f32[32,2048]{1,0:T(8,128)}, f32[32,2048]{1,0:T(8,128)}, u32[]{:S(2)}, u32[]{:S(2)}) collective-permute-start(f32[32,2048]{1,0:T(8,128)} %constant_dynamic-update-slice_fusion), channel_id=1, source_target_pairs={{0,7},{1,8},{2,9},{3,10},{4,11},{5,12},{6,13},{7,14},{8,15},{9,16}... | collective-permute-start | bytes 786440 | tf_op jit(solution)/shard_map/ppermute | solution.py:25
  11.3 3.2 %collective-permute-start.2 = (f32[32,2048]{1,0:T(8,128)}, f32[32,2048]{1,0:T(8,128)}, u32[]{:S(2)}, u32[]{:S(2)}) collective-permute-start(f32[32,2048]{1,0:T(8,128)} %constant_dynamic-update-slice_fusion), channel_id=1, source_target_pairs={{0,6},{1,7},{2,8},{3,9},{4,10},{5,11},{6,12},{7,13},{8,14},{9,15},... | collective-permute-start | bytes 786440 | tf_op jit(solution)/shard_map/ppermute | solution.py:25
  14.5 3.8 %collective-permute-start.3 = (f32[32,2048]{1,0:T(8,128)}, f32[32,2048]{1,0:T(8,128)}, u32[]{:S(2)}, u32[]{:S(2)}) collective-permute-start(f32[32,2048]{1,0:T(8,128)} %constant_dynamic-update-slice_fusion), channel_id=1, source_target_pairs={{0,5},{1,6},{2,7},{3,8},{4,9},{5,10},{6,11},{7,12},{8,13},{9,14},{... | collective-permute-start | bytes 786440 | tf_op jit(solution)/shard_map/ppermute | solution.py:25
  18.2 2.2 %copy.20 = f32[16,2048]{0,1:T(8,128)} copy(f32[16,2048]{1,0:T(8,128)} %points_ref.1) | data formatting | bytes 262144 | tf_op args[0]
  20.5 2.0 convolution_bitcast_fusion.1
  23.2 2.6 %gather_fusion = f32[256,16]{1,0:T(8,128)} fusion(f32[16,2048]{0,1:T(8,128)} %copy.20, s32[1024]{0:T(1024)S(1)} %pad_clamp_fusion.2), kind=kCustom, calls=%fused_computation | custom fusion | bytes 33792 | tf_op jit(solution)/shard_map/jit(_take)/gather | solution.py:205
  44.0 3.1 %collective-permute-done.21 = f32[32,512]{1,0:T(8,128)S(1)} collective-permute-done((f32[32,512]{1,0:T(8,128)S(1)}, f32[32,512]{1,0:T(8,128)S(1)}, u32[]{:S(2)}, u32[]{:S(2)}) %collective-permute-start.21) | collective-permute-done | bytes 65568 | tf_op jit(solution)/shard_map/ppermute | solution.py:31
  49.9 1.9 copy.26
  55.1 42.3 %all_gather.3 = f32[32,512]{0,1:T(8,128)S(1)} all-gather(f32[32,16]{0,1:T(8,128)S(1)} %pad_maximum_fusion.2), channel_id=1, replica_groups=mesh['leaf'=32] {'leaf'}, dimensions={1}, use_global_device_ids=true | all-gather | bytes 67584 | tf_op jit(solution)/shard_map/all_gather | solution.py:216
  104.5 4.9 %collective-permute-start.5 = (f32[32,2048]{1,0:T(8,128)}, f32[32,2048]{1,0:T(8,128)S(1)}, u32[]{:S(2)}, u32[]{:S(2)}) collective-permute-start(f32[32,2048]{1,0:T(8,128)} %constant_dynamic-update-slice_fusion), channel_id=1, source_target_pairs={{0,3},{1,4},{2,5},{3,6},{4,7},{5,8},{6,9},{7,10},{8,11},{9,12},{10... | collective-permute-start | bytes 786440 | tf_op jit(solution)/shard_map/ppermute | solution.py:25
  110.4 1.9 collective-permute-start.6
  113.3 3.4 %collective-permute-start.7 = (f32[32,2048]{1,0:T(8,128)}, f32[32,2048]{1,0:T(8,128)S(1)}, u32[]{:S(2)}, u32[]{:S(2)}) collective-permute-start(f32[32,2048]{1,0:T(8,128)} %constant_dynamic-update-slice_fusion), channel_id=1, source_target_pairs={{0,1},{1,2},{2,3},{3,4},{4,5},{5,6},{6,7},{7,8},{8,9},{9,10},{10,1... | collective-permute-start | bytes 786440 | tf_op jit(solution)/shard_map/ppermute | solution.py:25
  117.7 1.9 collective-permute-start.8
  120.6 2.7 %collective-permute-start.9 = (f32[32,2048]{1,0:T(8,128)}, f32[32,2048]{1,0:T(8,128)S(1)}, u32[]{:S(2)}, u32[]{:S(2)}) collective-permute-start(f32[32,2048]{1,0:T(8,128)} %constant_dynamic-update-slice_fusion), channel_id=1, source_target_pairs={{2,0},{3,1},{4,2},{5,3},{6,4},{7,5},{8,6},{9,7},{10,8},{11,9},{12,... | collective-permute-start | bytes 786440 | tf_op jit(solution)/shard_map/ppermute | solution.py:25
  123.4 1.9 collective-permute-start.10
  132.5 8.0 %collective-permute-done.10 = f32[32,2048]{1,0:T(8,128)S(1)} collective-permute-done((f32[32,2048]{1,0:T(8,128)}, f32[32,2048]{1,0:T(8,128)S(1)}, u32[]{:S(2)}, u32[]{:S(2)}) %collective-permute-start.10) | collective-permute-done | bytes 262176 | tf_op jit(solution)/shard_map/ppermute | solution.py:25
  141.8 2.0 collective-permute-start.23
  143.8 2.7 %collective-permute-done.23 = f32[16,256]{1,0:T(8,128)S(1)} collective-permute-done((f32[16,256]{1,0:T(8,128)S(1)}, f32[16,256]{1,0:T(8,128)S(1)}, u32[]{:S(2)}, u32[]{:S(2)}) %collective-permute-start.23) | collective-permute-done | bytes 16416 | tf_op jit(solution)/shard_map/ppermute | solution.py:31
  146.5 7.1 %collective-permute-start.24 = (f32[16,128]{1,0:T(8,128)S(1)}, f32[16,128]{1,0:T(8,128)S(1)}, u32[]{:S(2)}, u32[]{:S(2)}) collective-permute-start(f32[16,128]{1,0:T(8,128)S(1)} %slice_select_fusion.5), channel_id=1, source_target_pairs={{0,2},{1,3},{2,0},{3,1},{4,6},{5,7},{6,4},{7,5},{8,10},{9,11},{10,... | collective-permute-start | bytes 24584 | tf_op jit(solution)/shard_map/ppermute | solution.py:31
  155.4 3.8 %collective-permute-start.25 = (f32[16,64]{1,0:T(8,128)S(1)}, f32[16,64]{1,0:T(8,128)S(1)}, u32[]{:S(2)}, u32[]{:S(2)}) collective-permute-start(f32[16,64]{1,0:T(8,128)S(1)} %slice_select_fusion.4), channel_id=1, source_target_pairs={{0,1},{1,0},{2,3},{3,2},{4,5},{5,4},{6,7},{7,6},{8,9},{9,8},{10,11... | collective-permute-start | bytes 12296 | tf_op jit(solution)/shard_map/ppermute | solution.py:31
  160.7 1.8 collective-permute-start.26
  166.9 1.8 convolution_bitcast_fusion
  168.8 43.1 %near_tiles.1 = f32[16,2048]{1,0:T(8,128)} custom-call(s32[4,32]{1,0:T(4,128)S(1)} %broadcast_subtract_fusion.list_ref, s32[4]{0:T(128)S(1)} %copy-done.2, f32[16,2048]{1,0:T(8,128)S(1)} %copy-done.1, f32[17,32,2048]{2,1,0:T(8,128)S(1)} %bitcast_dynamic-update-slice_fusion.window_ref, f32[16,2048]{1,0:T(8,128)S(1)} %bitcast.78), custom_call_target="tpu_custom_call" | custom-call | tf_op jit(solution)/shard_map/near_tiles/pallas_call | solution.py:131
  (131 shorter events, 55.3 us)
Async XLA Ops:
  3.3 101.2 %collective-permute-start = (f32[32,2048]{1,0:T(8,128)}, f32[32,2048]{1,0:T(8,128)}, u32[]{:S(2)}, u32[]{:S(2)}) collective-permute-start(f32[32,2048]{1,0:T(8,128)} %constant_dynamic-update-slice_fusion), channel_id=1, source_target_pairs={{0,8},{1,9},{2,10},{3,11},{4,12},{5,13},{6,14},{7,15},{8,16},{9,17... | collective-permute-start | bytes 786440 | tf_op jit(solution)/shard_map/ppermute | solution.py:25
  7.2 103.2 %collective-permute-start.1 = (f32[32,2048]{1,0:T(8,128)}, f32[32,2048]{1,0:T(8,128)}, u32[]{:S(2)}, u32[]{:S(2)}) collective-permute-start(f32[32,2048]{1,0:T(8,128)} %constant_dynamic-update-slice_fusion), channel_id=1, source_target_pairs={{0,7},{1,8},{2,9},{3,10},{4,11},{5,12},{6,13},{7,14},{8,15},{9,16}... | collective-permute-start | bytes 786440 | tf_op jit(solution)/shard_map/ppermute | solution.py:25
  11.3 102.0 %collective-permute-start.2 = (f32[32,2048]{1,0:T(8,128)}, f32[32,2048]{1,0:T(8,128)}, u32[]{:S(2)}, u32[]{:S(2)}) collective-permute-start(f32[32,2048]{1,0:T(8,128)} %constant_dynamic-update-slice_fusion), channel_id=1, source_target_pairs={{0,6},{1,7},{2,8},{3,9},{4,10},{5,11},{6,12},{7,13},{8,14},{9,15},... | collective-permute-start | bytes 786440 | tf_op jit(solution)/shard_map/ppermute | solution.py:25
  14.5 103.2 %collective-permute-start.3 = (f32[32,2048]{1,0:T(8,128)}, f32[32,2048]{1,0:T(8,128)}, u32[]{:S(2)}, u32[]{:S(2)}) collective-permute-start(f32[32,2048]{1,0:T(8,128)} %constant_dynamic-update-slice_fusion), channel_id=1, source_target_pairs={{0,5},{1,6},{2,7},{3,8},{4,9},{5,10},{6,11},{7,12},{8,13},{9,14},{... | collective-permute-start | bytes 786440 | tf_op jit(solution)/shard_map/ppermute | solution.py:25
  29.3 3.6 %collective-permute-start.17 = (f32[32,512]{1,0:T(8,128)S(1)}, f32[32,512]{1,0:T(8,128)S(1)}, u32[]{:S(2)}, u32[]{:S(2)}) collective-permute-start(f32[32,512]{1,0:T(8,128)S(1)} %maximum_select_fusion.2), channel_id=1, source_target_pairs={{0,2},{1,3},{2,0},{3,1},{4,6},{5,7},{6,4},{7,5},{8,10},{9,11},{10,... | collective-permute-start | bytes 196616 | tf_op jit(solution)/shard_map/ppermute | solution.py:31
  41.1 2.8 %collective-permute-start.20 = (f32[32,256]{1,0:T(8,128)S(1)}, f32[32,256]{1,0:T(8,128)S(1)}, u32[]{:S(2)}, u32[]{:S(2)}) collective-permute-start(f32[32,256]{1,0:T(8,128)S(1)} %maximum_select_fusion.4), channel_id=1, source_target_pairs={{0,4},{1,5},{2,6},{3,7},{4,0},{5,1},{6,2},{7,3},{8,12},{9,13},{10,... | collective-permute-start | bytes 98312 | tf_op jit(solution)/shard_map/ppermute | solution.py:31
  43.9 3.2 %collective-permute-start.21 = (f32[32,512]{1,0:T(8,128)S(1)}, f32[32,512]{1,0:T(8,128)S(1)}, u32[]{:S(2)}, u32[]{:S(2)}) collective-permute-start(f32[32,512]{1,0:T(8,128)S(1)} %maximum_select_fusion.3), channel_id=1, source_target_pairs={{0,8},{1,9},{2,10},{3,11},{4,12},{5,13},{6,14},{7,15},{8,0},{9,1},... | collective-permute-start | bytes 196616 | tf_op jit(solution)/shard_map/ppermute | solution.py:31
  100.3 2.8 %collective-permute-start.22 = (f32[16,512]{1,0:T(8,128)S(1)}, f32[16,512]{1,0:T(8,128)S(1)}, u32[]{:S(2)}, u32[]{:S(2)}) collective-permute-start(f32[16,512]{1,0:T(8,128)S(1)} %slice_select_fusion.1), channel_id=1, source_target_pairs={{0,8},{1,9},{2,10},{3,11},{4,12},{5,13},{6,14},{7,15},{8,0},{9,1},... | collective-permute-start | bytes 98312 | tf_op jit(solution)/shard_map/ppermute | solution.py:31
  103.2 17.4 %collective-permute-start.4 = (f32[32,2048]{1,0:T(8,128)}, f32[32,2048]{1,0:T(8,128)S(1)}, u32[]{:S(2)}, u32[]{:S(2)}) collective-permute-start(f32[32,2048]{1,0:T(8,128)} %constant_dynamic-update-slice_fusion), channel_id=1, source_target_pairs={{0,4},{1,5},{2,6},{3,7},{4,8},{5,9},{6,10},{7,11},{8,12},{9,13},{1... | collective-permute-start | bytes 786440 | tf_op jit(solution)/shard_map/ppermute | solution.py:25
  104.5 18.9 %collective-permute-start.5 = (f32[32,2048]{1,0:T(8,128)}, f32[32,2048]{1,0:T(8,128)S(1)}, u32[]{:S(2)}, u32[]{:S(2)}) collective-permute-start(f32[32,2048]{1,0:T(8,128)} %constant_dynamic-update-slice_fusion), channel_id=1, source_target_pairs={{0,3},{1,4},{2,5},{3,6},{4,7},{5,8},{6,9},{7,10},{8,11},{9,12},{10... | collective-permute-start | bytes 786440 | tf_op jit(solution)/shard_map/ppermute | solution.py:25
  110.4 14.9 %collective-permute-start.6 = (f32[32,2048]{1,0:T(8,128)}, f32[32,2048]{1,0:T(8,128)S(1)}, u32[]{:S(2)}, u32[]{:S(2)}) collective-permute-start(f32[32,2048]{1,0:T(8,128)} %constant_dynamic-update-slice_fusion), channel_id=1, source_target_pairs={{0,2},{1,3},{2,4},{3,5},{4,6},{5,7},{6,8},{7,9},{8,10},{9,11},{10,... | collective-permute-start | bytes 786440 | tf_op jit(solution)/shard_map/ppermute | solution.py:25
  113.3 13.4 %collective-permute-start.7 = (f32[32,2048]{1,0:T(8,128)}, f32[32,2048]{1,0:T(8,128)S(1)}, u32[]{:S(2)}, u32[]{:S(2)}) collective-permute-start(f32[32,2048]{1,0:T(8,128)} %constant_dynamic-update-slice_fusion), channel_id=1, source_target_pairs={{0,1},{1,2},{2,3},{3,4},{4,5},{5,6},{6,7},{7,8},{8,9},{9,10},{10,1... | collective-permute-start | bytes 786440 | tf_op jit(solution)/shard_map/ppermute | solution.py:25
  117.7 11.3 %collective-permute-start.8 = (f32[32,2048]{1,0:T(8,128)}, f32[32,2048]{1,0:T(8,128)S(1)}, u32[]{:S(2)}, u32[]{:S(2)}) collective-permute-start(f32[32,2048]{1,0:T(8,128)} %constant_dynamic-update-slice_fusion), channel_id=1, source_target_pairs={{1,0},{2,1},{3,2},{4,3},{5,4},{6,5},{7,6},{8,7},{9,8},{10,9},{11,1... | collective-permute-start | bytes 786440 | tf_op jit(solution)/shard_map/ppermute | solution.py:25
  120.6 10.6 %collective-permute-start.9 = (f32[32,2048]{1,0:T(8,128)}, f32[32,2048]{1,0:T(8,128)S(1)}, u32[]{:S(2)}, u32[]{:S(2)}) collective-permute-start(f32[32,2048]{1,0:T(8,128)} %constant_dynamic-update-slice_fusion), channel_id=1, source_target_pairs={{2,0},{3,1},{4,2},{5,3},{6,4},{7,5},{8,6},{9,7},{10,8},{11,9},{12,... | collective-permute-start | bytes 786440 | tf_op jit(solution)/shard_map/ppermute | solution.py:25
  123.4 17.1 %collective-permute-start.10 = (f32[32,2048]{1,0:T(8,128)}, f32[32,2048]{1,0:T(8,128)S(1)}, u32[]{:S(2)}, u32[]{:S(2)}) collective-permute-start(f32[32,2048]{1,0:T(8,128)} %constant_dynamic-update-slice_fusion), channel_id=1, source_target_pairs={{3,0},{4,1},{5,2},{6,3},{7,4},{8,5},{9,6},{10,7},{11,8},{12,9},{13... | collective-permute-start | bytes 786440 | tf_op jit(solution)/shard_map/ppermute | solution.py:25
  125.3 16.4 %collective-permute-start.11 = (f32[32,2048]{1,0:T(8,128)}, f32[32,2048]{1,0:T(8,128)S(1)}, u32[]{:S(2)}, u32[]{:S(2)}) collective-permute-start(f32[32,2048]{1,0:T(8,128)} %constant_dynamic-update-slice_fusion), channel_id=1, source_target_pairs={{4,0},{5,1},{6,2},{7,3},{8,4},{9,5},{10,6},{11,7},{12,8},{13,9},{1... | collective-permute-start | bytes 786440 | tf_op jit(solution)/shard_map/ppermute | solution.py:25
  126.7 26.9 %collective-permute-start.12 = (f32[32,2048]{1,0:T(8,128)}, f32[32,2048]{1,0:T(8,128)S(1)}, u32[]{:S(2)}, u32[]{:S(2)}) collective-permute-start(f32[32,2048]{1,0:T(8,128)} %constant_dynamic-update-slice_fusion), channel_id=1, source_target_pairs={{5,0},{6,1},{7,2},{8,3},{9,4},{10,5},{11,6},{12,7},{13,8},{14,9},{... | collective-permute-start | bytes 786440 | tf_op jit(solution)/shard_map/ppermute | solution.py:25
  129.0 30.2 %collective-permute-start.13 = (f32[32,2048]{1,0:T(8,128)}, f32[32,2048]{1,0:T(8,128)S(1)}, u32[]{:S(2)}, u32[]{:S(2)}) collective-permute-start(f32[32,2048]{1,0:T(8,128)} %constant_dynamic-update-slice_fusion), channel_id=1, source_target_pairs={{6,0},{7,1},{8,2},{9,3},{10,4},{11,5},{12,6},{13,7},{14,8},{15,9},... | collective-permute-start | bytes 786440 | tf_op jit(solution)/shard_map/ppermute | solution.py:25
  131.2 31.3 %collective-permute-start.14 = (f32[32,2048]{1,0:T(8,128)}, f32[32,2048]{1,0:T(8,128)S(1)}, u32[]{:S(2)}, u32[]{:S(2)}) collective-permute-start(f32[32,2048]{1,0:T(8,128)} %constant_dynamic-update-slice_fusion), channel_id=1, source_target_pairs={{7,0},{8,1},{9,2},{10,3},{11,4},{12,5},{13,6},{14,7},{15,8},{16,9}... | collective-permute-start | bytes 786440 | tf_op jit(solution)/shard_map/ppermute | solution.py:25
  140.4 24.7 %collective-permute-start.15 = (f32[32,2048]{1,0:T(8,128)}, f32[32,2048]{1,0:T(8,128)S(1)}, u32[]{:S(2)}, u32[]{:S(2)}) collective-permute-start(f32[32,2048]{1,0:T(8,128)} %constant_dynamic-update-slice_fusion), channel_id=1, source_target_pairs={{8,0},{9,1},{10,2},{11,3},{12,4},{13,5},{14,6},{15,7},{16,8},{17,9... | collective-permute-start | bytes 786440 | tf_op jit(solution)/shard_map/ppermute | solution.py:25
  141.8 4.7 %collective-permute-start.23 = (f32[16,256]{1,0:T(8,128)S(1)}, f32[16,256]{1,0:T(8,128)S(1)}, u32[]{:S(2)}, u32[]{:S(2)}) collective-permute-start(f32[16,256]{1,0:T(8,128)S(1)} %slice_select_fusion.3), channel_id=1, source_target_pairs={{0,4},{1,5},{2,6},{3,7},{4,0},{5,1},{6,2},{7,3},{8,12},{9,13},{10,... | collective-permute-start | bytes 49160 | tf_op jit(solution)/shard_map/ppermute | solution.py:31
  146.5 8.9 %collective-permute-start.24 = (f32[16,128]{1,0:T(8,128)S(1)}, f32[16,128]{1,0:T(8,128)S(1)}, u32[]{:S(2)}, u32[]{:S(2)}) collective-permute-start(f32[16,128]{1,0:T(8,128)S(1)} %slice_select_fusion.5), channel_id=1, source_target_pairs={{0,2},{1,3},{2,0},{3,1},{4,6},{5,7},{6,4},{7,5},{8,10},{9,11},{10,... | collective-permute-start | bytes 24584 | tf_op jit(solution)/shard_map/ppermute | solution.py:31
  155.4 4.6 %collective-permute-start.25 = (f32[16,64]{1,0:T(8,128)S(1)}, f32[16,64]{1,0:T(8,128)S(1)}, u32[]{:S(2)}, u32[]{:S(2)}) collective-permute-start(f32[16,64]{1,0:T(8,128)S(1)} %slice_select_fusion.4), channel_id=1, source_target_pairs={{0,1},{1,0},{2,3},{3,2},{4,5},{5,4},{6,7},{7,6},{8,9},{9,8},{10,11... | collective-permute-start | bytes 12296 | tf_op jit(solution)/shard_map/ppermute | solution.py:31
  160.7 3.4 %collective-permute-start.26 = (f32[16,512]{1,0:T(8,128)S(1)}, f32[16,512]{1,0:T(8,128)S(1)}, u32[]{:S(2)}, u32[]{:S(2)}) collective-permute-start(f32[16,512]{1,0:T(8,128)S(1)} %slice_select_fusion), channel_id=1, source_target_pairs={{0,2},{1,3},{2,0},{3,1},{4,6},{5,7},{6,4},{7,5},{8,10},{9,11},{10,... | collective-permute-start | bytes 98312 | tf_op jit(solution)/shard_map/ppermute | solution.py:31
  (14 other events, 278.9 us)
